TPU v7x, 256 devices: a whole 4x4x8 slice. The times are simulated.
256 devices in a mesh: gx: 8 (over x, core), gy: 8 (over z), gz: 4 (over y).
Axes of the slice: x: 4, y: 4, z: 8, core: 2. Of those that a mesh axis runs over, the one named last changes fastest.
Arguments:
- spectrum: bfloat16 [256, 256, 32, 256], P('gx', 'gy', 'gz'), may hold values from 0.049804688 to 2
- wind_east: float32 [256, 256, 32], P('gx', 'gy', 'gz'), may hold values from -0.45 to 0.45
- wind_north: float32 [256, 256, 32], P('gx', 'gy', 'gz'), may hold values from -0.45 to 0.45
- fall_rate: float32 [32, 256], P('gz'), may hold values from 0.006 to 12
- cloud_cells: int32 [8, 8, 4, 64, 16], P('gx', 'gy', 'gz'), may hold values from 0 to 8191, as said below
- block_target: int32 [8, 8, 4, 64], P(None, None, 'gz'), may hold values from 0 to 64, as said below
- pair_inputs: bfloat16 [256, 2048], replicated, may hold values from -0.375 to 0.375
- pair_outputs: bfloat16 [1024, 256], replicated, may hold values from -0.1875 to 0.1875
- loss_kernel: bfloat16 [256, 256], replicated, may hold values from 0 to 0.00390625
- fragments: bfloat16 [256, 256], replicated, may hold values from 0 to 0.0078125
Outputs:
- settled: bfloat16 [256, 256, 32, 256], P('gx', 'gy', 'gz')
Inputs may be any that keep to these rules, and one draw needn't show every extreme that they name: `cloud_cells`: entry [i, j, k, b, :] lists the local cell numbers (x * 32 + y) * 8 + z of block b of the device at mesh index (i, j, k); the 1024 entries of one device are distinct. `block_target`: entry [i, j, k, b] below 64 is the flat index i2 * (devices along gy) + j2 of the device (i2, j2, k) that works on block b of device (i, j, k); 64 marks a block without cloud. In each gz index the cloudy blocks number 64 * 32 in all, a device holds 1 to 64 of them, every device of the plane is named exactly 32 times, and by at most 1 block of any one device.
All inputs are finite; a program needn't handle non-finite values.
Results may differ from a plain program's by a relative error of at most 0.0032.
Values may be sent and summed in bfloat16 or wider, within the bound.
No kernel may reach another device: no remote copies, remote signals or barrier semaphores. Data moves between devices by JAX's collectives and lax.ppermute only.
A program may use at most 128 MiB of HBM per device.

v0:
```python
import jax
import jax.numpy as jnp
from jax import lax
from jax.sharding import PartitionSpec as P


def padded_2(x, sides, width):
    edges = {}
    for axis, dim in sides:
        size, length = (lax.axis_size(axis), x.shape[dim])
        up = [(i, (i + 1) % size) for i in range(size)]
        last = lax.slice_in_dim(x, length - width, length, axis=dim)
        initial = lax.slice_in_dim(x, 0, width, axis=dim)
        edges[dim] = (
            lax.ppermute(last, axis, up),
            lax.ppermute(initial, axis, [(b, a) for a, b in up]),
        )
    done = []
    for _, dim in sides:
        low, high = edges[dim]
        around = [(width, width) if d in done else (0, 0) for d in range(x.ndim)]
        x = jnp.concatenate([jnp.pad(low, around), x, jnp.pad(high, around)], axis=dim)
        done.append(dim)
    return x


def collide(cloud_rows, pair_inputs, pair_outputs, loss_kernel, fragments):
    pair_count = pair_outputs.shape[0]
    linear = jnp.dot(cloud_rows, pair_inputs, preferred_element_type=jnp.float32)
    products = (linear[:, :pair_count] * linear[:, pair_count:]).astype(jnp.bfloat16)
    decline = jnp.dot(cloud_rows, loss_kernel, preferred_element_type=jnp.float32)
    losses = cloud_rows.astype(jnp.float32) * decline
    gained = jnp.dot(products, pair_outputs, preferred_element_type=jnp.float32)
    gained = gained + jnp.dot(
        losses.astype(jnp.bfloat16), fragments, preferred_element_type=jnp.float32
    )
    return (gained - losses).astype(jnp.bfloat16)


def advect(spectrum, wind_east, wind_north):
    padded = padded_2(spectrum, (("gx", 0), ("gy", 1)), 1)
    centre = spectrum.astype(jnp.float32)
    from_west = padded[:-2, 1:-1].astype(jnp.float32)
    from_east = padded[2:, 1:-1].astype(jnp.float32)
    from_south = padded[1:-1, :-2].astype(jnp.float32)
    from_north = padded[1:-1, 2:].astype(jnp.float32)
    east_rate = wind_east[..., None]
    north_rate = wind_north[..., None]
    return (
        centre
        - jnp.maximum(east_rate, 0.0) * (centre - from_west)
        - jnp.minimum(east_rate, 0.0) * (from_east - centre)
        - jnp.maximum(north_rate, 0.0) * (centre - from_south)
        - jnp.minimum(north_rate, 0.0) * (from_north - centre)
    )


def segment_maps(fall_rate):
    levels, channels = fall_rate.shape
    inverse = 1.0 / (1.0 + fall_rate)
    rows = [None] * levels
    gains = [None] * levels
    above_row = jnp.zeros((levels, channels), jnp.float32)
    above_gain = jnp.ones((channels,), jnp.float32)
    level_ids = jnp.arange(levels)[:, None]
    for level_index in reversed(range(levels)):
        own_row = jnp.where(level_ids == level_index, 1.0, 0.0).astype(jnp.float32)
        row = inverse[level_index][None, :] * (own_row + above_row)
        gain = inverse[level_index] * above_gain
        rows[level_index] = row
        gains[level_index] = gain
        above_row = fall_rate[level_index][None, :] * row
        above_gain = fall_rate[level_index] * gain
    return (jnp.stack(rows, axis=0), jnp.stack(gains, axis=0), above_row, above_gain)


def body(
    spectrum,
    wind_east,
    wind_north,
    fall_rate,
    cloud_cells,
    block_target,
    pair_inputs,
    pair_outputs,
    loss_kernel,
    fragments,
):
    size_x, size_y, size_z, channels = spectrum.shape
    number_of_cells = size_x * size_y * size_z
    advected = advect(spectrum, wind_east, wind_north)
    flat_cells = advected.reshape(number_of_cells, channels)
    blocks_total = cloud_cells.shape[3]
    block_cells = cloud_cells.shape[4]
    cell_ids = cloud_cells.reshape(blocks_total * block_cells)
    blocks = flat_cells[cell_ids].astype(jnp.bfloat16).reshape(blocks_total, block_cells, channels)
    plane_size = lax.axis_size("gx") * lax.axis_size("gy")
    own_index = lax.axis_index("gx") * lax.axis_size("gy") + lax.axis_index("gy")
    routes = block_target.reshape(plane_size, blocks_total)
    own_targets = lax.dynamic_index_in_dim(routes, own_index, 0, keepdims=False)
    active = own_targets < plane_size
    zero_value = jnp.zeros((), jnp.bfloat16)
    computed = collide(
        blocks.reshape(-1, channels), pair_inputs, pair_outputs, loss_kernel, fragments
    )
    tendency = jnp.where(
        active[:, None, None], computed.reshape(blocks_total, block_cells, channels), zero_value
    )
    moist_field = (
        flat_cells.at[cell_ids]
        .add(tendency.reshape(-1, channels).astype(jnp.float32))
        .reshape(size_x, size_y, size_z, channels)
    )
    level_rows, level_gains, out_row, carried_gain = segment_maps(fall_rate)
    local_values = jnp.zeros((size_x, size_y, size_z, channels), jnp.float32)
    inflow = jnp.zeros((size_x, size_y, channels), jnp.float32)
    for source in range(size_z):
        source_level = moist_field[:, :, source : source + 1, :]
        local_values = local_values + source_level * level_rows[:, source, :]
        inflow = inflow + source_level[:, :, 0, :] * out_row[source]
    all_flux, all_gain = (
        lax.all_gather(inflow[None].astype(jnp.bfloat16), "gz", axis=0, tiled=True).astype(
            jnp.float32
        ),
        lax.all_gather(carried_gain[None].astype(jnp.bfloat16), "gz", axis=0, tiled=True).astype(
            jnp.float32
        ),
    )
    height = lax.axis_size("gz")
    own_level = lax.axis_index("gz")
    incoming = jnp.zeros_like(inflow)
    for upper in reversed(range(height)):
        incoming = jnp.where(
            upper > own_level, all_flux[upper] + all_gain[upper] * incoming, incoming
        )
    return (local_values + incoming[:, :, None, :] * level_gains).astype(jnp.bfloat16)


def solution(mesh):
    in_specs = (
        P("gx", "gy", "gz", None),
        P("gx", "gy", "gz"),
        P("gx", "gy", "gz"),
        P("gz", None),
        P("gx", "gy", "gz", None, None),
        P(None, None, "gz", None),
        P(),
        P(),
        P(),
        P(),
    )
    out_specs = P("gx", "gy", "gz", None)
    return jax.shard_map(body, mesh=mesh, in_specs=in_specs, out_specs=out_specs, check_vma=False)
```

profile of v0, /device:TPU:1, one launch (start us, length us, event | category | flops | bytes accessed | tf_op | source)
XLA Modules:
  0.0 160.9 jit_solution(9245047635911674080)
XLA Ops:
  6.5 1.8 %fusion.58 = (bf16[1,32,8,256]{3,2,1,0:T(8,128)(2,1)}, bf16[1,32,8,256]{3,2,1,0:T(8,128)(2,1)}) fusion(bf16[32,32,8,256]{3,2,1,0:T(8,128)(2,1)} %param.10), kind=kLoop, calls=%fused_computation.129 | loop fusion | bytes 524288 | tf_op jit(solution)/shard_map/slice | solution.py:13
  8.3 2.6 %collective-permute-start = (bf16[1,32,8,256]{3,2,1,0:T(8,128)(2,1)}, bf16[1,32,8,256]{3,2,1,0:T(8,128)(2,1)S(1)}, u32[]{:S(2)}, u32[]{:S(2)}) collective-permute-start(bf16[1,32,8,256]{3,2,1,0:T(8,128)(2,1)} %get-tuple-element.24), channel_id=1, source_target_pairs={{0,32},{32,64},{64,96},{96,128},{128,160},{160,192},{192,224},{224... | collective-permute-start | bytes 393224 | tf_op jit(solution)/shard_map/ppermute | solution.py:15
  10.9 0.6 collective-permute-start.1
  11.5 1.7 %fusion.57 = (bf16[32,1,8,256]{3,2,1,0:T(8,128)(2,1)}, bf16[32,1,8,256]{3,2,1,0:T(8,128)(2,1)}) fusion(bf16[32,32,8,256]{3,2,1,0:T(8,128)(2,1)} %param.10), kind=kLoop, calls=%fused_computation.128 | loop fusion | bytes 524288 | tf_op jit(solution)/shard_map/slice | solution.py:12
  13.2 1.0 collective-permute-start.2
  14.2 3.9 %collective-permute-start.3 = (bf16[32,1,8,256]{3,2,1,0:T(8,128)(2,1)}, bf16[32,1,8,256]{3,2,1,0:T(8,128)(2,1)}, u32[]{:S(2)}, u32[]{:S(2)}) collective-permute-start(bf16[32,1,8,256]{3,2,1,0:T(8,128)(2,1)} %get-tuple-element.22), channel_id=1, source_target_pairs={{4,0},{8,4},{12,8},{16,12},{20,16},{24,20},{28,24},{0,28},{5,1},{9... | collective-permute-start | bytes 393224 | tf_op jit(solution)/shard_map/ppermute | solution.py:16
  18.2 0.7 add_divide_fusion
  18.9 0.6 fusion.62
  19.5 1.6 %convert_bitcast_fusion = (bf16[1,1,256]{2,1,0:T(2,128)(2,1)}, f32[1,256]{1,0:T(1,128)}, f32[1,256]{1,0:T(1,128)}, f32[1,256]{1,0:T(1,128)}, f32[1,256]{1,0:T(1,...) fusion(f32[8,256]{1,0:T(8,128)} %param.13, ...), kind=kLoop, calls=%fused_computation.119 | loop fusion | flops 4096 | bytes 27136
  21.1 1.6 fusion.61
  22.7 0.6 compare_select_fusion.1
  23.2 0.5 compare_select_fusion.3
  23.8 0.6 compare_select_fusion.5
  24.4 0.6 compare_select_fusion.7
  24.9 0.9 broadcast_maximum_fusion.1
  25.9 0.2 copy.39
  26.1 0.2 copy.40
  26.3 0.9 broadcast_maximum_fusion
  27.2 0.2 copy.41
  27.5 0.2 copy.42
  27.7 0.8 copy.43
  28.5 0.1 reshape.2557
  28.6 0.7 compare_bitcast_fusion
  29.3 0.1 broadcast_in_dim.53
  29.4 0.6 broadcast_in_dim.54
  30.0 1.6 constant_dynamic-update-slice_fusion.10
  31.6 0.8 multiply_multiply_fusion.1
  32.4 0.6 fusion.60
  33.0 1.4 constant_dynamic-update-slice_fusion.9
  34.5 0.6 broadcast_clamp_fusion
  35.1 2.5 %constant_dynamic-update-slice_fusion.1 = bf16[34,32,8,256]{3,2,1,0:T(8,128)(2,1)S(1)} fusion(bf16[34,32,8,256]{3,2,1,0:T(8,128)(2,1)S(1)} %constant_dynamic-update-slice_fusion.2, bf16[32,32,8,256]{3,2,1,0:T(8,128)(2,1)} %param.10), kind=kLoop, calls=%fused_computation.76 | loop fusion | bytes 8388608
  37.6 12.5 %fusion.3 = f32[32,32,8,256]{3,2,1,0:T(8,128)} fusion(bf16[32,32,8,256]{3,2,1,0:T(8,128)(2,1)S(1)} %copy-done.1, bf16[34,32,8,256]{3,2,1,0:T(8,128)(2,1)S(1)} %constant_dynamic-update-slice_fusion, bf16[32,1,8,256]{3,2,1,0:T(8,128)(2,1)} %collective-permute-done.3, bf16[32,1,8,256]{3,2,1,0:T(8,128)(2,1)} %collective-permute-done.2, ...), kind=kLoop, calls=%fused_computation.10 | loop fusion | flops 73400320 | bytes 17694720 | tf_op jit(solution)/shard_map/sub | solution.py:50
  50.1 7.4 %gather_fusion = bf16[1024,256]{1,0:T(8,128)(2,1)S(1)} fusion(f32[8192,256]{1,0:T(8,128)} %bitcast.160, s32[1024]{0:T(1024)} %broadcast_clamp_fusion), kind=kCustom, calls=%fused_computation | custom fusion | bytes 1052672 | tf_op jit(solution)/shard_map/gather | solution.py:96
  57.5 0.3 fusion.65
  57.8 1.3 fusion.64
  59.1 0.3 fusion.46
  59.4 1.0 fusion.26
  60.5 12.7 %scatter_fusion = f32[8192,256]{1,0:T(8,128)} fusion(f32[8192,256]{1,0:T(8,128)} %bitcast.161, s32[1024]{0:T(1024)S(1)} %bitcast.215, f32[1024,256]{1,0:T(8,128)S(1)} %fusion.26), kind=kCustom, calls=%fused_computation.1 | custom fusion | flops 262144 | bytes 3149824 | tf_op jit(solution)/shard_map/scatter-add | solution.py:111
  73.3 30.4 %fusion.56 = (f32[32,32,1,256]{3,2,1,0:T(1,128)S(1)}, f32[32,32,1,256]{3,2,1,0:T(1,128)S(1)}, f32[32,32,1,256]{3,2,1,0:T(1,128)S(1)}, f32[32,32,1,256]{3,2,1,0:T...) fusion(f32[32,32,8,256]{3,2,1,0:T(8,128)} %bitcast.162), kind=kLoop, calls=%fused_computation.127 | loop fusion | bytes 16777216 | tf_op jit(solution)/shard_map/slice | solution.py:118
  103.9 0.7 copy-done.2
  104.6 0.4 copy-done.4
  105.0 0.3 copy-done.6
  105.3 0.4 copy-done.7
  105.7 0.3 copy-done.8
  106.0 0.3 copy-done.9
  106.4 1.9 %fusion.38 = bf16[1,32,32,256]{3,2,1,0:T(8,128)(2,1)} fusion(f32[32,32,1,256]{3,2,1,0:T(1,128)S(1)} %get-tuple-element.20, f32[32,32,1,256]{3,2,1,0:T(1,128)S(1)} %get-tuple-element.14, f32[32,32,1,256]{3,2,1,0:T(1,128)S(1)} %get-tuple-element.15, f32[32,32,1,256]{3,2,1,0:T(1,128)S(1)} %get-tuple-element.16, f32[32,32,1,256]{3,2,1,0:T(1,128)S(1)} %get-tuple-element.17, ...), kind=kLoop, calls=%fused_computation.45 | loop fusion | flops 4194304 | bytes 8921088 | tf_op jit(solution)/shard_map/convert_element_type | solution.py:122
  108.3 0.0 all-gather.3.cloned.1.call-update
  108.5 0.1 constant_dynamic-update-slice_fusion.8
  108.6 8.0 %all-gather = bf16[4,1,256]{2,1,0:T(2,128)(2,1)S(1)} all-gather(bf16[1,1,256]{2,1,0:T(2,128)(2,1)S(1)} %copy-done.53), channel_id=1, replica_groups=mesh['gx'=8,'gy'=8,'gz'=4] {'gz'}, dimensions={0}, use_global_device_ids=true | all-gather | bytes 2560 | tf_op jit(solution)/shard_map/all_gather | solution.py:125
  116.5 0.1 constant_dynamic-update-slice_fusion.7
  116.6 0.1 constant_dynamic-update-slice_fusion.6
  116.7 0.1 constant_dynamic-update-slice_fusion.5
  116.8 0.1 constant_dynamic-update-slice_fusion.4
  116.9 0.1 constant_dynamic-update-slice_fusion.3
  117.2 3.3 %copy_bitcast_fusion.6 = (f32[32,32,256]{2,1,0:T(8,128)}, f32[32,32,256]{2,1,0:T(8,128)}) fusion(f32[32,32,1,256]{3,2,1,0:T(1,128)} %copy-done.9, f32[32,32,1,256]{3,2,1,0:T(1,128)} %copy-done.8), kind=kLoop, calls=%fused_computation.66 | loop fusion | bytes 4194304 | tf_op jit(solution)/shard_map/mul | solution.py:119
  120.5 3.3 %copy_bitcast_fusion.4 = (f32[32,32,256]{2,1,0:T(8,128)}, f32[32,32,256]{2,1,0:T(8,128)}) fusion(f32[32,32,1,256]{3,2,1,0:T(1,128)} %copy-done.6, f32[32,32,1,256]{3,2,1,0:T(1,128)} %copy-done.7), kind=kLoop, calls=%fused_computation.64 | loop fusion | bytes 4194304 | tf_op jit(solution)/shard_map/mul | solution.py:119
  123.8 1.5 copy_bitcast_fusion.2
  125.3 1.5 copy_bitcast_fusion
  126.8 15.7 %all-gather.3.cloned.1.call-done = bf16[4,32,32,256]{3,2,1,0:T(8,128)(2,1)} async-done(((bf16[1,32,32,256]{3,2,1,0:T(8,128)(2,1)}), bf16[4,32,32,256]{3,2,1,0:T(8,128)(2,1)}) %all-gather.3.cloned.1.call-update) | async-done | bytes 2097168 | tf_op jit(solution)/shard_map/all_gather | solution.py:122
  142.5 2.2 %convert_element_type.73 = f32[4,32,32,256]{3,2,1,0:T(8,128)S(1)} convert(bf16[4,32,32,256]{3,2,1,0:T(8,128)(2,1)} %all-gather.3.cloned.1.call-done) | non-fusion elementwise | flops 1048576 | bytes 6291456 | tf_op jit(solution)/shard_map/convert_element_type | solution.py:122
  144.8 0.6 fusion.36
  145.4 0.2 copy-done.16
  145.6 0.3 copy-done.17
  146.0 8.1 %add_convert_fusion = bf16[32,32,8,256]{3,2,1,0:T(8,128)(2,1)} fusion(f32[8,256]{1,0:T(8,128)S(1)} %stack.5, f32[32,32,256]{2,1,0:T(8,128)S(1)} %fusion.36, f32[8,256]{1,0:T(8,128)S(1)} %bitcast.226, f32[32,32,256]{2,1,0:T(8,128)S(1)} %copy-done.16, f32[8,256]{1,0:T(8,128)S(1)} %bitcast.227, f32[32,32,256]{2,1,0:T(8,128)S(1)} %copy-done.17, ...), kind=kLoop, calls=%fused_computation.16 | loop fusion | flops 37748736 | bytes 13705216 | tf_op jit(solution)/shard_map/convert_element_type | solution.py:136
  (121 shorter events, 0.4 us)
Async XLA Ops:
  6.5 51.3 %copy-start = (bf16[256,2048]{1,0:T(8,128)(2,1)S(1)}, bf16[256,2048]{1,0:T(8,128)(2,1)}, u32[]{:S(2)}) copy-start(bf16[256,2048]{1,0:T(8,128)(2,1)} %param.16) | copy-start | bytes 3145732
  6.5 136.0 %all-gather.3.cloned.1.call-start = ((), (), s32[]{:S(2)}) async-start(), calls=%async_computation | async-start | bytes 2621440 | tf_op jit(solution)/shard_map/all_gather | solution.py:122
  8.3 26.8 %collective-permute-start = (bf16[1,32,8,256]{3,2,1,0:T(8,128)(2,1)}, bf16[1,32,8,256]{3,2,1,0:T(8,128)(2,1)S(1)}, u32[]{:S(2)}, u32[]{:S(2)}) collective-permute-start(bf16[1,32,8,256]{3,2,1,0:T(8,128)(2,1)} %get-tuple-element.24), channel_id=1, source_target_pairs={{0,32},{32,64},{64,96},{96,128},{128,160},{160,192},{192,224},{224... | collective-permute-start | bytes 393224 | tf_op jit(solution)/shard_map/ppermute | solution.py:15
  10.9 26.6 %collective-permute-start.1 = (bf16[1,32,8,256]{3,2,1,0:T(8,128)(2,1)}, bf16[1,32,8,256]{3,2,1,0:T(8,128)(2,1)S(1)}, u32[]{:S(2)}, u32[]{:S(2)}) collective-permute-start(bf16[1,32,8,256]{3,2,1,0:T(8,128)(2,1)} %get-tuple-element.23), channel_id=1, source_target_pairs={{32,0},{64,32},{96,64},{128,96},{160,128},{192,160},{224,192},{0,2... | collective-permute-start | bytes 393224 | tf_op jit(solution)/shard_map/ppermute | solution.py:16
  13.2 24.4 %collective-permute-start.2 = (bf16[32,1,8,256]{3,2,1,0:T(8,128)(2,1)}, bf16[32,1,8,256]{3,2,1,0:T(8,128)(2,1)}, u32[]{:S(2)}, u32[]{:S(2)}) collective-permute-start(bf16[32,1,8,256]{3,2,1,0:T(8,128)(2,1)} %get-tuple-element.21), channel_id=1, source_target_pairs={{0,4},{4,8},{8,12},{12,16},{16,20},{20,24},{24,28},{28,0},{1,5},{5... | collective-permute-start | bytes 393224 | tf_op jit(solution)/shard_map/ppermute | solution.py:15
  14.2 23.4 %collective-permute-start.3 = (bf16[32,1,8,256]{3,2,1,0:T(8,128)(2,1)}, bf16[32,1,8,256]{3,2,1,0:T(8,128)(2,1)}, u32[]{:S(2)}, u32[]{:S(2)}) collective-permute-start(bf16[32,1,8,256]{3,2,1,0:T(8,128)(2,1)} %get-tuple-element.22), channel_id=1, source_target_pairs={{4,0},{8,4},{12,8},{16,12},{20,16},{24,20},{28,24},{0,28},{5,1},{9... | collective-permute-start | bytes 393224 | tf_op jit(solution)/shard_map/ppermute | solution.py:16
  28.6 9.0 %copy-start.26 = (s32[1024,1]{0,1:T(1,128)}, s32[1024,1]{0,1:T(1,128)S(1)}, u32[]{:S(2)}) copy-start(s32[1024,1]{0,1:T(1,128)S(1)} %compare_select_fusion) | copy-start | bytes 12292
  30.0 7.6 %copy-start.1 = (bf16[32,32,8,256]{3,2,1,0:T(8,128)(2,1)S(1)}, bf16[32,32,8,256]{3,2,1,0:T(8,128)(2,1)}, u32[]{:S(2)}) copy-start(bf16[32,32,8,256]{3,2,1,0:T(8,128)(2,1)} %param.10) | copy-start | bytes 12582916
  37.6 19.9 %copy-start.19 = (bf16[256,256]{1,0:T(8,128)(2,1)S(1)}, bf16[256,256]{1,0:T(8,128)(2,1)}, u32[]{:S(2)}) copy-start(bf16[256,256]{1,0:T(8,128)(2,1)} %param.18) | copy-start | bytes 393220
  50.1 9.0 %copy-start.20 = (bf16[256,256]{1,0:T(8,128)(2,1)S(1)}, bf16[256,256]{1,0:T(8,128)(2,1)}, u32[]{:S(2)}) copy-start(bf16[256,256]{1,0:T(8,128)(2,1)} %param.19) | copy-start | bytes 393220
  57.5 1.9 %copy-start.18 = (bf16[1024,256]{1,0:T(8,128)(2,1)S(1)}, bf16[1024,256]{1,0:T(8,128)(2,1)}, u32[]{:S(2)}) copy-start(bf16[1024,256]{1,0:T(8,128)(2,1)} %param.17) | copy-start | bytes 1572868
  57.5 1.9 %copy-start.45 = (pred[1024]{0:T(1024)(128)(4,1)S(1)}, pred[1024]{0:T(1024)(128)(4,1)}, u32[]{:S(2)}) copy-start(pred[1024]{0:T(1024)(128)(4,1)} %broadcast_in_dim.54) | copy-start | bytes 3076
  59.1 1.4 copy-start.27
  73.2 33.1 %copy-start.37 = (f32[1,256]{1,0:T(1,128)S(1)}, f32[1,256]{1,0:T(1,128)}, u32[]{:S(2)}) copy-start(f32[1,256]{1,0:T(1,128)} %get-tuple-element.37) | copy-start | bytes 3076
  73.2 33.1 %copy-start.38 = (f32[1,256]{1,0:T(1,128)S(1)}, f32[1,256]{1,0:T(1,128)}, u32[]{:S(2)}) copy-start(f32[1,256]{1,0:T(1,128)} %get-tuple-element.38) | copy-start | bytes 3076
  73.2 33.1 %copy-start.39 = (f32[1,256]{1,0:T(1,128)S(1)}, f32[1,256]{1,0:T(1,128)}, u32[]{:S(2)}) copy-start(f32[1,256]{1,0:T(1,128)} %get-tuple-element.39) | copy-start | bytes 3076
  73.2 33.1 %copy-start.40 = (f32[1,256]{1,0:T(1,128)S(1)}, f32[1,256]{1,0:T(1,128)}, u32[]{:S(2)}) copy-start(f32[1,256]{1,0:T(1,128)} %get-tuple-element.40) | copy-start | bytes 3076
  73.2 33.1 %copy-start.41 = (f32[1,256]{1,0:T(1,128)S(1)}, f32[1,256]{1,0:T(1,128)}, u32[]{:S(2)}) copy-start(f32[1,256]{1,0:T(1,128)} %get-tuple-element.41) | copy-start | bytes 3076
  73.2 33.1 %copy-start.42 = (f32[1,256]{1,0:T(1,128)S(1)}, f32[1,256]{1,0:T(1,128)}, u32[]{:S(2)}) copy-start(f32[1,256]{1,0:T(1,128)} %get-tuple-element.42) | copy-start | bytes 3076
  73.3 33.1 %copy-start.43 = (f32[1,256]{1,0:T(1,128)S(1)}, f32[1,256]{1,0:T(1,128)}, u32[]{:S(2)}) copy-start(f32[1,256]{1,0:T(1,128)} %get-tuple-element.43) | copy-start | bytes 3076
  73.3 33.1 %copy-start.44 = (f32[1,256]{1,0:T(1,128)S(1)}, f32[1,256]{1,0:T(1,128)}, u32[]{:S(2)}) copy-start(f32[1,256]{1,0:T(1,128)} %get-tuple-element.44) | copy-start | bytes 3076
  103.7 1.0 copy-start.2
  103.7 1.3 copy-start.4
  103.7 1.6 %copy-start.6 = (f32[32,32,1,256]{3,2,1,0:T(1,128)}, f32[32,32,1,256]{3,2,1,0:T(1,128)S(1)}, u32[]{:S(2)}) copy-start(f32[32,32,1,256]{3,2,1,0:T(1,128)S(1)} %get-tuple-element.17) | copy-start | bytes 3145732
  103.7 2.0 %copy-start.7 = (f32[32,32,1,256]{3,2,1,0:T(1,128)}, f32[32,32,1,256]{3,2,1,0:T(1,128)S(1)}, u32[]{:S(2)}) copy-start(f32[32,32,1,256]{3,2,1,0:T(1,128)S(1)} %get-tuple-element.18) | copy-start | bytes 3145732
  103.7 2.3 %copy-start.8 = (f32[32,32,1,256]{3,2,1,0:T(1,128)}, f32[32,32,1,256]{3,2,1,0:T(1,128)S(1)}, u32[]{:S(2)}) copy-start(f32[32,32,1,256]{3,2,1,0:T(1,128)S(1)} %get-tuple-element.13) | copy-start | bytes 3145732
  103.7 2.6 %copy-start.9 = (f32[32,32,1,256]{3,2,1,0:T(1,128)}, f32[32,32,1,256]{3,2,1,0:T(1,128)S(1)}, u32[]{:S(2)}) copy-start(f32[32,32,1,256]{3,2,1,0:T(1,128)S(1)} %get-tuple-element.19) | copy-start | bytes 3145732
  103.7 4.6 %copy-start.21 = (f32[8,8,256]{2,1,0:T(8,128)S(1)}, f32[8,8,256]{2,1,0:T(8,128)}, u32[]{:S(2)}) copy-start(f32[8,8,256]{2,1,0:T(8,128)} %constant_dynamic-update-slice_fusion.9) | copy-start | bytes 196612
  103.7 4.6 %copy-start.22 = (f32[1,256]{1,0:T(1,128)S(1)}, f32[1,256]{1,0:T(1,128)}, u32[]{:S(2)}) copy-start(f32[1,256]{1,0:T(1,128)} %get-tuple-element.58) | copy-start | bytes 3076
  103.7 4.6 %copy-start.23 = (f32[1,256]{1,0:T(1,128)S(1)}, f32[1,256]{1,0:T(1,128)}, u32[]{:S(2)}) copy-start(f32[1,256]{1,0:T(1,128)} %get-tuple-element.50) | copy-start | bytes 3076
  103.8 4.6 %copy-start.24 = (f32[1,256]{1,0:T(1,128)S(1)}, f32[1,256]{1,0:T(1,128)}, u32[]{:S(2)}) copy-start(f32[1,256]{1,0:T(1,128)} %get-tuple-element.59) | copy-start | bytes 3076
  103.8 4.6 %copy-start.25 = (f32[8]{0:T(128)S(1)}, f32[8]{0:T(128)}, u32[]{:S(2)}) copy-start(f32[8]{0:T(128)} %get-tuple-element.64) | copy-start | bytes 100
  103.8 4.6 %copy-start.28 = (f32[1,256]{1,0:T(1,128)S(1)}, f32[1,256]{1,0:T(1,128)}, u32[]{:S(2)}) copy-start(f32[1,256]{1,0:T(1,128)} %get-tuple-element.51) | copy-start | bytes 3076
  103.8 4.6 %copy-start.29 = (f32[1,256]{1,0:T(1,128)S(1)}, f32[1,256]{1,0:T(1,128)}, u32[]{:S(2)}) copy-start(f32[1,256]{1,0:T(1,128)} %get-tuple-element.60) | copy-start | bytes 3076
  103.8 4.6 %copy-start.30 = (f32[8]{0:T(128)S(1)}, f32[8]{0:T(128)}, u32[]{:S(2)}) copy-start(f32[8]{0:T(128)} %get-tuple-element.65) | copy-start | bytes 100
  103.8 4.6 %copy-start.31 = (f32[1,256]{1,0:T(1,128)S(1)}, f32[1,256]{1,0:T(1,128)}, u32[]{:S(2)}) copy-start(f32[1,256]{1,0:T(1,128)} %get-tuple-element.52) | copy-start | bytes 3076
  103.8 4.6 %copy-start.32 = (f32[1,256]{1,0:T(1,128)S(1)}, f32[1,256]{1,0:T(1,128)}, u32[]{:S(2)}) copy-start(f32[1,256]{1,0:T(1,128)} %get-tuple-element.55) | copy-start | bytes 3076
  103.8 4.6 %copy-start.33 = (f32[8]{0:T(128)S(1)}, f32[8]{0:T(128)}, u32[]{:S(2)}) copy-start(f32[8]{0:T(128)} %get-tuple-element.66) | copy-start | bytes 100
  103.8 4.6 %copy-start.34 = (f32[8]{0:T(128)S(1)}, f32[8]{0:T(128)}, u32[]{:S(2)}) copy-start(f32[8]{0:T(128)} %get-tuple-element.67) | copy-start | bytes 100
  103.8 4.6 %copy-start.35 = (f32[8]{0:T(128)S(1)}, f32[8]{0:T(128)}, u32[]{:S(2)}) copy-start(f32[8]{0:T(128)} %get-tuple-element.68) | copy-start | bytes 100
  103.8 4.6 %copy-start.36 = (f32[8]{0:T(128)S(1)}, f32[8]{0:T(128)}, u32[]{:S(2)}) copy-start(f32[8]{0:T(128)} %get-tuple-element.69) | copy-start | bytes 100
  103.9 4.7 %copy-start.53 = (bf16[1,1,256]{2,1,0:T(2,128)(2,1)S(1)}, bf16[1,1,256]{2,1,0:T(2,128)(2,1)}, u32[]{:S(2)}) copy-start(bf16[1,1,256]{2,1,0:T(2,128)(2,1)} %get-tuple-element.5) | copy-start | bytes 1540
  103.9 13.2 %copy-start.46 = (f32[1,256]{1,0:T(1,128)S(1)}, f32[1,256]{1,0:T(1,128)}, u32[]{:S(2)}) copy-start(f32[1,256]{1,0:T(1,128)} %get-tuple-element.6) | copy-start | bytes 3076
  103.9 13.2 %copy-start.47 = (f32[1,256]{1,0:T(1,128)S(1)}, f32[1,256]{1,0:T(1,128)}, u32[]{:S(2)}) copy-start(f32[1,256]{1,0:T(1,128)} %get-tuple-element.7) | copy-start | bytes 3076
  103.9 13.2 %copy-start.48 = (f32[1,256]{1,0:T(1,128)S(1)}, f32[1,256]{1,0:T(1,128)}, u32[]{:S(2)}) copy-start(f32[1,256]{1,0:T(1,128)} %get-tuple-element.8) | copy-start | bytes 3076
  103.9 13.2 %copy-start.49 = (f32[1,256]{1,0:T(1,128)S(1)}, f32[1,256]{1,0:T(1,128)}, u32[]{:S(2)}) copy-start(f32[1,256]{1,0:T(1,128)} %get-tuple-element.9) | copy-start | bytes 3076
  103.9 13.2 %copy-start.50 = (f32[1,256]{1,0:T(1,128)S(1)}, f32[1,256]{1,0:T(1,128)}, u32[]{:S(2)}) copy-start(f32[1,256]{1,0:T(1,128)} %get-tuple-element.10) | copy-start | bytes 3076
  103.9 13.2 %copy-start.51 = (f32[1,256]{1,0:T(1,128)S(1)}, f32[1,256]{1,0:T(1,128)}, u32[]{:S(2)}) copy-start(f32[1,256]{1,0:T(1,128)} %get-tuple-element.11) | copy-start | bytes 3076
  103.9 13.2 %copy-start.52 = (f32[1,256]{1,0:T(1,128)S(1)}, f32[1,256]{1,0:T(1,128)}, u32[]{:S(2)}) copy-start(f32[1,256]{1,0:T(1,128)} %get-tuple-element.12) | copy-start | bytes 3076
  117.2 6.6 %copy-start.3 = (f32[32,32,1,256]{3,2,1,0:T(1,128)S(1)}, f32[32,32,1,256]{3,2,1,0:T(1,128)}, u32[]{:S(2)}) copy-start(f32[32,32,1,256]{3,2,1,0:T(1,128)} %copy-done.2) | copy-start | bytes 3145732
  117.2 6.6 %copy-start.5 = (f32[32,32,1,256]{3,2,1,0:T(1,128)S(1)}, f32[32,32,1,256]{3,2,1,0:T(1,128)}, u32[]{:S(2)}) copy-start(f32[32,32,1,256]{3,2,1,0:T(1,128)} %copy-done.4) | copy-start | bytes 3145732
  126.8 18.6 %copy-start.10 = (f32[32,32,256]{2,1,0:T(8,128)S(1)}, f32[32,32,256]{2,1,0:T(8,128)}, u32[]{:S(2)}) copy-start(f32[32,32,256]{2,1,0:T(8,128)} %get-tuple-element.78) | copy-start | bytes 3145732
  126.8 18.6 %copy-start.11 = (f32[32,32,256]{2,1,0:T(8,128)S(1)}, f32[32,32,256]{2,1,0:T(8,128)}, u32[]{:S(2)}) copy-start(f32[32,32,256]{2,1,0:T(8,128)} %get-tuple-element.79) | copy-start | bytes 3145732
  142.5 2.9 %copy-start.12 = (f32[32,32,256]{2,1,0:T(8,128)S(1)}, f32[32,32,256]{2,1,0:T(8,128)}, u32[]{:S(2)}) copy-start(f32[32,32,256]{2,1,0:T(8,128)} %get-tuple-element.76) | copy-start | bytes 3145732
  142.5 2.9 %copy-start.13 = (f32[32,32,256]{2,1,0:T(8,128)S(1)}, f32[32,32,256]{2,1,0:T(8,128)}, u32[]{:S(2)}) copy-start(f32[32,32,256]{2,1,0:T(8,128)} %get-tuple-element.77) | copy-start | bytes 3145732
  142.5 2.9 %copy-start.14 = (f32[32,32,256]{2,1,0:T(8,128)S(1)}, f32[32,32,256]{2,1,0:T(8,128)}, u32[]{:S(2)}) copy-start(f32[32,32,256]{2,1,0:T(8,128)} %get-tuple-element.74) | copy-start | bytes 3145732
  142.5 2.9 %copy-start.15 = (f32[32,32,256]{2,1,0:T(8,128)S(1)}, f32[32,32,256]{2,1,0:T(8,128)}, u32[]{:S(2)}) copy-start(f32[32,32,256]{2,1,0:T(8,128)} %get-tuple-element.75) | copy-start | bytes 3145732
  142.5 3.1 %copy-start.16 = (f32[32,32,256]{2,1,0:T(8,128)S(1)}, f32[32,32,256]{2,1,0:T(8,128)}, u32[]{:S(2)}) copy-start(f32[32,32,256]{2,1,0:T(8,128)} %get-tuple-element.72) | copy-start | bytes 3145732
  142.5 3.4 %copy-start.17 = (f32[32,32,256]{2,1,0:T(8,128)S(1)}, f32[32,32,256]{2,1,0:T(8,128)}, u32[]{:S(2)}) copy-start(f32[32,32,256]{2,1,0:T(8,128)} %get-tuple-element.73) | copy-start | bytes 3145732
Sparse Core Ops, SparseCore 0:
  108.5 34.0 all-gather.2
where the time goes:
time: 162 us; the launch traced here: 161 us
  local copies, waits for them, and re-layouts  61.7 us (38%)
  other arithmetic  50.1 us (31%)
  waiting for transfers between devices  15.7 us (10%)
  between operations  14.3 us (9%)
  starting transfers between devices  8.19 us (5%)
  blocking collectives  7.95 us (5%)
  matrix products  2.91 us (2%)
    slice x1, local copies, waits for them, and re-layouts, body(): source_level = moist_field[:, :, source:source + 1, :]  30.4 us
    all_gather x1, waiting for transfers between devices, body(): lax.all_gather(inflow[None].astype(jnp.bfloat16), 'gz', axis=0, tiled=True)  15.7 us
    scatter-add x1, other arithmetic, body(): moist_field = flat_cells.at[cell_ids].add(tendency.reshape(-1, channels)....  12.7 us
    sub x1, other arithmetic, advect(): centre - jnp.maximum(east_rate, 0.0) * (centre - from_west)  12.5 us
    mul x4, local copies, waits for them, and re-layouts, body(): local_values = local_values + source_level * level_rows[:, source, :]  9.6 us
    convert_element_type x1, other arithmetic, body(): (local_values + incoming[:, :, None, :] * level_gains).astype(jnp.bfloat16)  8.12 us
    all_gather x1, blocking collectives, body(): lax.all_gather(carried_gain[None].astype(jnp.bfloat16), 'gz', axis=0, til...  7.95 us
    gather x1, local copies, waits for them, and re-layouts, body(): flat_cells[cell_ids].astype(jnp.bfloat16)  7.36 us
  transfers between devices with their start and end apart: 5, of which 1 were waited for; matrix products, arithmetic and copies ran while one was open for 19% of the time, Pallas kernels for 0%

commit v1 on v0

--- a/solution.py
+++ b/solution.py
@@ -122,9 +122,15 @@
         lax.all_gather(inflow[None].astype(jnp.bfloat16), "gz", axis=0, tiled=True).astype(
             jnp.float32
         ),
-        lax.all_gather(carried_gain[None].astype(jnp.bfloat16), "gz", axis=0, tiled=True).astype(
-            jnp.float32
-        ),
+        jnp.concatenate(
+            lax.all_to_all(
+                jnp.stack([carried_gain[None].astype(jnp.bfloat16)] * lax.axis_size("gz")),
+                "gz",
+                0,
+                0,
+            ),
+            axis=0,
+        ).astype(jnp.float32),
     )
     height = lax.axis_size("gz")
     own_level = lax.axis_index("gz")

time: 162 us -> 168 us (1.037)
  waiting for transfers between devices: 15.7 us -> 23.8 us
  blocking collectives: 7.95 us -> 0 us
  starting transfers between devices: 8.19 us -> 12.4 us
  local copies, waits for them, and re-layouts: 61.7 us -> 63.5 us
    all_gather x1, waiting for transfers between devices: 15.7 us -> 23.7 us  [body(): lax.all_gather(inflow[None].astype(jnp.bfloat16), 'gz', axis=0, tiled=True)]
    all_gather x1 -> x0, blocking collectives: 7.95 us -> none  [body(): lax.all_gather(carried_gain[None].astype(jnp.bfloat16), 'gz', axis=0, til...]
    all_to_all x0 -> x1, starting transfers between devices: none -> 4.18 us  [body(): lax.all_to_all(jnp.stack([carried_gain[None].astype(jnp.bfloat16)] * lax....]
    unnamed x8 -> x7, other arithmetic: 5.05 us -> 3.44 us
  transfers between devices with their start and end apart: 5 -> 6, of which waited for: 1 -> 1; matrix products, arithmetic and copies ran while one was open for 19% -> 60% of each run, Pallas kernels for 0% -> 0%
where the time goes in v1:
time: 168 us
  local copies, waits for them, and re-layouts  63.5 us (38%)
  other arithmetic  50.7 us (30%)
  waiting for transfers between devices  23.8 us (14%)
  between operations  14.3 us (9%)
  starting transfers between devices  12.4 us (7%)
  matrix products  2.91 us (2%)
    slice x1, local copies, waits for them, and re-layouts, body(): source_level = moist_field[:, :, source:source + 1, :]  30.5 us
    all_gather x1, waiting for transfers between devices, body(): lax.all_gather(inflow[None].astype(jnp.bfloat16), 'gz', axis=0, tiled=True)  23.7 us
    scatter-add x1, other arithmetic, body(): moist_field = flat_cells.at[cell_ids].add(tendency.reshape(-1, channels)....  12.7 us
    sub x1, other arithmetic, advect(): centre - jnp.maximum(east_rate, 0.0) * (centre - from_west)  12.5 us
    mul x4, local copies, waits for them, and re-layouts, body(): local_values = local_values + source_level * level_rows[:, source, :]  9.43 us
    convert_element_type x1, other arithmetic, body(): (local_values + incoming[:, :, None, :] * level_gains).astype(jnp.bfloat16)  8.12 us
    unnamed x119, local copies, waits for them, and re-layouts  7.64 us
    gather x1, local copies, waits for them, and re-layouts, body(): flat_cells[cell_ids].astype(jnp.bfloat16)  7.36 us
  transfers between devices with their start and end apart: 6, of which 1 were waited for; matrix products, arithmetic and copies ran while one was open for 60% of the time, Pallas kernels for 0%

profile of v1, /device:TPU:1, one launch (start us, length us, event | category | flops | bytes accessed | tf_op | source)
XLA Modules:
  0.0 167.6 jit_solution(12176542309992120883)
XLA Ops:
  6.5 1.8 %fusion.58 = (bf16[1,32,8,256]{3,2,1,0:T(8,128)(2,1)}, bf16[1,32,8,256]{3,2,1,0:T(8,128)(2,1)}) fusion(bf16[32,32,8,256]{3,2,1,0:T(8,128)(2,1)} %param.10), kind=kLoop, calls=%fused_computation.129 | loop fusion | bytes 524288 | tf_op jit(solution)/shard_map/slice | solution.py:13
  8.3 2.6 %collective-permute-start = (bf16[1,32,8,256]{3,2,1,0:T(8,128)(2,1)}, bf16[1,32,8,256]{3,2,1,0:T(8,128)(2,1)S(1)}, u32[]{:S(2)}, u32[]{:S(2)}) collective-permute-start(bf16[1,32,8,256]{3,2,1,0:T(8,128)(2,1)} %get-tuple-element.24), channel_id=1, source_target_pairs={{0,32},{32,64},{64,96},{96,128},{128,160},{160,192},{192,224},{224... | collective-permute-start | bytes 393224 | tf_op jit(solution)/shard_map/ppermute | solution.py:15
  10.9 0.6 collective-permute-start.1
  11.6 1.7 %fusion.57 = (bf16[32,1,8,256]{3,2,1,0:T(8,128)(2,1)}, bf16[32,1,8,256]{3,2,1,0:T(8,128)(2,1)}) fusion(bf16[32,32,8,256]{3,2,1,0:T(8,128)(2,1)} %param.10), kind=kLoop, calls=%fused_computation.128 | loop fusion | bytes 524288 | tf_op jit(solution)/shard_map/slice | solution.py:12
  13.3 1.0 collective-permute-start.2
  14.3 3.9 %collective-permute-start.3 = (bf16[32,1,8,256]{3,2,1,0:T(8,128)(2,1)}, bf16[32,1,8,256]{3,2,1,0:T(8,128)(2,1)}, u32[]{:S(2)}, u32[]{:S(2)}) collective-permute-start(bf16[32,1,8,256]{3,2,1,0:T(8,128)(2,1)} %get-tuple-element.22), channel_id=1, source_target_pairs={{4,0},{8,4},{12,8},{16,12},{20,16},{24,20},{28,24},{0,28},{5,1},{9... | collective-permute-start | bytes 393224 | tf_op jit(solution)/shard_map/ppermute | solution.py:16
  18.2 0.7 add_divide_fusion
  18.9 1.6 convert_reduce_fusion
  20.5 0.5 broadcast.1864
  21.1 0.7 reduce.2
  21.7 0.5 reshape.2592
  22.3 4.2 %all-to-all-start = ((bf16[4,2,128]{2,1,0:T(2,128)(2,1)}), bf16[4,2,128]{2,1,0:T(2,128)(2,1)}, u32[]{:S(2)}, u32[]{:S(2)}) async-start(bf16[4,2,128]{2,1,0:T(2,128)(2,1)} %reshape.2592), calls=%async_computation | async-start | bytes 4096 | tf_op jit(solution)/shard_map/all_to_all | solution.py:126
  26.5 0.6 fusion.62
  27.1 1.6 fusion.61
  28.7 0.5 compare_select_fusion.1
  29.2 0.6 compare_select_fusion.3
  29.8 0.5 compare_select_fusion.5
  30.3 0.5 compare_select_fusion.7
  30.9 0.9 broadcast_maximum_fusion.1
  31.8 0.2 copy.39
  32.0 0.2 copy.40
  32.2 0.9 broadcast_maximum_fusion
  33.2 0.2 copy.41
  33.4 0.2 copy.42
  33.6 0.8 copy.43
  34.4 0.1 reshape.2572
  34.5 0.7 compare_bitcast_fusion
  35.2 0.1 broadcast_in_dim.53
  35.3 0.6 broadcast_in_dim.54
  35.9 1.6 constant_dynamic-update-slice_fusion.10
  37.5 0.9 multiply_multiply_fusion.1
  38.4 0.6 fusion.60
  39.0 1.4 constant_dynamic-update-slice_fusion.9
  40.4 0.6 broadcast_clamp_fusion
  41.0 2.5 %constant_dynamic-update-slice_fusion.1 = bf16[34,32,8,256]{3,2,1,0:T(8,128)(2,1)S(1)} fusion(bf16[34,32,8,256]{3,2,1,0:T(8,128)(2,1)S(1)} %constant_dynamic-update-slice_fusion.2, bf16[32,32,8,256]{3,2,1,0:T(8,128)(2,1)} %param.10), kind=kLoop, calls=%fused_computation.76 | loop fusion | bytes 8388608
  43.6 12.5 %fusion.3 = f32[32,32,8,256]{3,2,1,0:T(8,128)} fusion(bf16[32,32,8,256]{3,2,1,0:T(8,128)(2,1)S(1)} %copy-done.1, bf16[34,32,8,256]{3,2,1,0:T(8,128)(2,1)S(1)} %constant_dynamic-update-slice_fusion, bf16[32,1,8,256]{3,2,1,0:T(8,128)(2,1)} %collective-permute-done.3, bf16[32,1,8,256]{3,2,1,0:T(8,128)(2,1)} %collective-permute-done.2, ...), kind=kLoop, calls=%fused_computation.10 | loop fusion | flops 73400320 | bytes 17694720 | tf_op jit(solution)/shard_map/sub | solution.py:50
  56.1 7.4 %gather_fusion = bf16[1024,256]{1,0:T(8,128)(2,1)S(1)} fusion(f32[8192,256]{1,0:T(8,128)} %bitcast.158, s32[1024]{0:T(1024)} %broadcast_clamp_fusion), kind=kCustom, calls=%fused_computation | custom fusion | bytes 1052672 | tf_op jit(solution)/shard_map/gather | solution.py:96
  63.5 0.3 fusion.65
  63.8 1.3 fusion.64
  65.1 0.3 fusion.46
  65.4 1.0 fusion.26
  66.5 12.7 %scatter_fusion = f32[8192,256]{1,0:T(8,128)} fusion(f32[8192,256]{1,0:T(8,128)} %bitcast.159, s32[1024]{0:T(1024)S(1)} %bitcast.213, f32[1024,256]{1,0:T(8,128)S(1)} %fusion.26), kind=kCustom, calls=%fused_computation.1 | custom fusion | flops 262144 | bytes 3149824 | tf_op jit(solution)/shard_map/scatter-add | solution.py:111
  79.2 30.5 %fusion.56 = (f32[32,32,1,256]{3,2,1,0:T(1,128)S(1)}, f32[32,32,1,256]{3,2,1,0:T(1,128)S(1)}, f32[32,32,1,256]{3,2,1,0:T(1,128)S(1)}, f32[32,32,1,256]{3,2,1,0:T...) fusion(f32[32,32,8,256]{3,2,1,0:T(8,128)} %bitcast.160), kind=kLoop, calls=%fused_computation.127 | loop fusion | bytes 16777216 | tf_op jit(solution)/shard_map/slice | solution.py:118
  110.0 0.7 copy-done.2
  110.7 0.4 copy-done.4
  111.0 0.3 copy-done.6
  111.4 0.4 copy-done.7
  111.8 0.3 copy-done.8
  112.1 0.3 copy-done.9
  112.5 1.9 %fusion.38 = bf16[1,32,32,256]{3,2,1,0:T(8,128)(2,1)} fusion(f32[32,32,1,256]{3,2,1,0:T(1,128)S(1)} %get-tuple-element.20, f32[32,32,1,256]{3,2,1,0:T(1,128)S(1)} %get-tuple-element.14, f32[32,32,1,256]{3,2,1,0:T(1,128)S(1)} %get-tuple-element.15, f32[32,32,1,256]{3,2,1,0:T(1,128)S(1)} %get-tuple-element.16, f32[32,32,1,256]{3,2,1,0:T(1,128)S(1)} %get-tuple-element.17, ...), kind=kLoop, calls=%fused_computation.45 | loop fusion | flops 4194304 | bytes 8921088 | tf_op jit(solution)/shard_map/convert_element_type | solution.py:122
  114.6 0.1 constant_dynamic-update-slice_fusion.8
  114.6 0.1 constant_dynamic-update-slice_fusion.7
  114.7 0.1 constant_dynamic-update-slice_fusion.6
  115.3 0.7 reshape.2593
  116.0 3.3 %copy_bitcast_fusion.6 = (f32[32,32,256]{2,1,0:T(8,128)}, f32[32,32,256]{2,1,0:T(8,128)}) fusion(f32[32,32,1,256]{3,2,1,0:T(1,128)} %copy-done.9, f32[32,32,1,256]{3,2,1,0:T(1,128)} %copy-done.8), kind=kLoop, calls=%fused_computation.66 | loop fusion | bytes 4194304 | tf_op jit(solution)/shard_map/mul | solution.py:119
  119.3 3.1 %copy_bitcast_fusion.4 = (f32[32,32,256]{2,1,0:T(8,128)}, f32[32,32,256]{2,1,0:T(8,128)}) fusion(f32[32,32,1,256]{3,2,1,0:T(1,128)} %copy-done.6, f32[32,32,1,256]{3,2,1,0:T(1,128)} %copy-done.7), kind=kLoop, calls=%fused_computation.64 | loop fusion | bytes 4194304 | tf_op jit(solution)/shard_map/mul | solution.py:119
  122.5 1.5 copy_bitcast_fusion.2
  124.0 1.5 copy_bitcast_fusion
  125.5 23.7 %all-gather.2.cloned.1.call-done = bf16[4,32,32,256]{3,2,1,0:T(8,128)(2,1)} async-done(((bf16[1,32,32,256]{3,2,1,0:T(8,128)(2,1)}), bf16[4,32,32,256]{3,2,1,0:T(8,128)(2,1)}) %all-gather.2.cloned.1.call-update) | async-done | bytes 2097168 | tf_op jit(solution)/shard_map/all_gather | solution.py:122
  149.2 2.2 %convert_element_type.76 = f32[4,32,32,256]{3,2,1,0:T(8,128)S(1)} convert(bf16[4,32,32,256]{3,2,1,0:T(8,128)(2,1)} %all-gather.2.cloned.1.call-done) | non-fusion elementwise | flops 1048576 | bytes 6291456 | tf_op jit(solution)/shard_map/convert_element_type | solution.py:122
  151.5 0.6 fusion.36
  152.1 0.2 copy-done.16
  152.3 0.3 copy-done.17
  152.6 8.1 %add_convert_fusion = bf16[32,32,8,256]{3,2,1,0:T(8,128)(2,1)} fusion(f32[8,256]{1,0:T(8,128)S(1)} %stack.8, f32[32,32,256]{2,1,0:T(8,128)S(1)} %fusion.36, f32[8,256]{1,0:T(8,128)S(1)} %bitcast.224, f32[32,32,256]{2,1,0:T(8,128)S(1)} %copy-done.16, f32[8,256]{1,0:T(8,128)S(1)} %bitcast.225, f32[32,32,256]{2,1,0:T(8,128)S(1)} %copy-done.17, ...), kind=kLoop, calls=%fused_computation.16 | loop fusion | flops 37748736 | bytes 13705216 | tf_op jit(solution)/shard_map/convert_element_type | solution.py:142
  (125 shorter events, 0.6 us)
Async XLA Ops:
  6.5 57.3 %copy-start = (bf16[256,2048]{1,0:T(8,128)(2,1)S(1)}, bf16[256,2048]{1,0:T(8,128)(2,1)}, u32[]{:S(2)}) copy-start(bf16[256,2048]{1,0:T(8,128)(2,1)} %param.16) | copy-start | bytes 3145732
  8.3 32.7 %collective-permute-start = (bf16[1,32,8,256]{3,2,1,0:T(8,128)(2,1)}, bf16[1,32,8,256]{3,2,1,0:T(8,128)(2,1)S(1)}, u32[]{:S(2)}, u32[]{:S(2)}) collective-permute-start(bf16[1,32,8,256]{3,2,1,0:T(8,128)(2,1)} %get-tuple-element.24), channel_id=1, source_target_pairs={{0,32},{32,64},{64,96},{96,128},{128,160},{160,192},{192,224},{224... | collective-permute-start | bytes 393224 | tf_op jit(solution)/shard_map/ppermute | solution.py:15
  10.9 32.6 %collective-permute-start.1 = (bf16[1,32,8,256]{3,2,1,0:T(8,128)(2,1)}, bf16[1,32,8,256]{3,2,1,0:T(8,128)(2,1)S(1)}, u32[]{:S(2)}, u32[]{:S(2)}) collective-permute-start(bf16[1,32,8,256]{3,2,1,0:T(8,128)(2,1)} %get-tuple-element.23), channel_id=1, source_target_pairs={{32,0},{64,32},{96,64},{128,96},{160,128},{192,160},{224,192},{0,2... | collective-permute-start | bytes 393224 | tf_op jit(solution)/shard_map/ppermute | solution.py:16
  13.3 30.3 %collective-permute-start.2 = (bf16[32,1,8,256]{3,2,1,0:T(8,128)(2,1)}, bf16[32,1,8,256]{3,2,1,0:T(8,128)(2,1)}, u32[]{:S(2)}, u32[]{:S(2)}) collective-permute-start(bf16[32,1,8,256]{3,2,1,0:T(8,128)(2,1)} %get-tuple-element.21), channel_id=1, source_target_pairs={{0,4},{4,8},{8,12},{12,16},{16,20},{20,24},{24,28},{28,0},{1,5},{5... | collective-permute-start | bytes 393224 | tf_op jit(solution)/shard_map/ppermute | solution.py:15
  14.3 29.3 %collective-permute-start.3 = (bf16[32,1,8,256]{3,2,1,0:T(8,128)(2,1)}, bf16[32,1,8,256]{3,2,1,0:T(8,128)(2,1)}, u32[]{:S(2)}, u32[]{:S(2)}) collective-permute-start(bf16[32,1,8,256]{3,2,1,0:T(8,128)(2,1)} %get-tuple-element.22), channel_id=1, source_target_pairs={{4,0},{8,4},{12,8},{16,12},{20,16},{24,20},{28,24},{0,28},{5,1},{9... | collective-permute-start | bytes 393224 | tf_op jit(solution)/shard_map/ppermute | solution.py:16
  22.3 93.0 %all-to-all-start = ((bf16[4,2,128]{2,1,0:T(2,128)(2,1)}), bf16[4,2,128]{2,1,0:T(2,128)(2,1)}, u32[]{:S(2)}, u32[]{:S(2)}) async-start(bf16[4,2,128]{2,1,0:T(2,128)(2,1)} %reshape.2592), calls=%async_computation | async-start | bytes 4096 | tf_op jit(solution)/shard_map/all_to_all | solution.py:126
  26.4 122.7 %all-gather.2.cloned.1.call-start = ((), (), s32[]{:S(2)}) async-start(), calls=%async_computation.1 | async-start | bytes 2621440 | tf_op jit(solution)/shard_map/all_gather | solution.py:122
  34.5 9.0 %copy-start.26 = (s32[1024,1]{0,1:T(1,128)}, s32[1024,1]{0,1:T(1,128)S(1)}, u32[]{:S(2)}) copy-start(s32[1024,1]{0,1:T(1,128)S(1)} %compare_select_fusion) | copy-start | bytes 12292
  35.9 7.7 %copy-start.1 = (bf16[32,32,8,256]{3,2,1,0:T(8,128)(2,1)S(1)}, bf16[32,32,8,256]{3,2,1,0:T(8,128)(2,1)}, u32[]{:S(2)}) copy-start(bf16[32,32,8,256]{3,2,1,0:T(8,128)(2,1)} %param.10) | copy-start | bytes 12582916
  43.6 19.9 %copy-start.19 = (bf16[256,256]{1,0:T(8,128)(2,1)S(1)}, bf16[256,256]{1,0:T(8,128)(2,1)}, u32[]{:S(2)}) copy-start(bf16[256,256]{1,0:T(8,128)(2,1)} %param.18) | copy-start | bytes 393220
  56.1 9.0 %copy-start.20 = (bf16[256,256]{1,0:T(8,128)(2,1)S(1)}, bf16[256,256]{1,0:T(8,128)(2,1)}, u32[]{:S(2)}) copy-start(bf16[256,256]{1,0:T(8,128)(2,1)} %param.19) | copy-start | bytes 393220
  63.5 1.9 %copy-start.18 = (bf16[1024,256]{1,0:T(8,128)(2,1)S(1)}, bf16[1024,256]{1,0:T(8,128)(2,1)}, u32[]{:S(2)}) copy-start(bf16[1024,256]{1,0:T(8,128)(2,1)} %param.17) | copy-start | bytes 1572868
  63.5 1.9 %copy-start.45 = (pred[1024]{0:T(1024)(128)(4,1)S(1)}, pred[1024]{0:T(1024)(128)(4,1)}, u32[]{:S(2)}) copy-start(pred[1024]{0:T(1024)(128)(4,1)} %broadcast_in_dim.54) | copy-start | bytes 3076
  65.1 1.4 copy-start.27
  79.2 33.2 %copy-start.37 = (f32[1,256]{1,0:T(1,128)S(1)}, f32[1,256]{1,0:T(1,128)}, u32[]{:S(2)}) copy-start(f32[1,256]{1,0:T(1,128)} %get-tuple-element.37) | copy-start | bytes 3076
  79.2 33.2 %copy-start.38 = (f32[1,256]{1,0:T(1,128)S(1)}, f32[1,256]{1,0:T(1,128)}, u32[]{:S(2)}) copy-start(f32[1,256]{1,0:T(1,128)} %get-tuple-element.38) | copy-start | bytes 3076
  79.2 33.2 %copy-start.39 = (f32[1,256]{1,0:T(1,128)S(1)}, f32[1,256]{1,0:T(1,128)}, u32[]{:S(2)}) copy-start(f32[1,256]{1,0:T(1,128)} %get-tuple-element.39) | copy-start | bytes 3076
  79.2 33.2 %copy-start.40 = (f32[1,256]{1,0:T(1,128)S(1)}, f32[1,256]{1,0:T(1,128)}, u32[]{:S(2)}) copy-start(f32[1,256]{1,0:T(1,128)} %get-tuple-element.40) | copy-start | bytes 3076
  79.2 33.2 %copy-start.41 = (f32[1,256]{1,0:T(1,128)S(1)}, f32[1,256]{1,0:T(1,128)}, u32[]{:S(2)}) copy-start(f32[1,256]{1,0:T(1,128)} %get-tuple-element.41) | copy-start | bytes 3076
  79.2 33.2 %copy-start.42 = (f32[1,256]{1,0:T(1,128)S(1)}, f32[1,256]{1,0:T(1,128)}, u32[]{:S(2)}) copy-start(f32[1,256]{1,0:T(1,128)} %get-tuple-element.42) | copy-start | bytes 3076
  79.2 33.2 %copy-start.43 = (f32[1,256]{1,0:T(1,128)S(1)}, f32[1,256]{1,0:T(1,128)}, u32[]{:S(2)}) copy-start(f32[1,256]{1,0:T(1,128)} %get-tuple-element.43) | copy-start | bytes 3076
  79.2 33.2 %copy-start.44 = (f32[1,256]{1,0:T(1,128)S(1)}, f32[1,256]{1,0:T(1,128)}, u32[]{:S(2)}) copy-start(f32[1,256]{1,0:T(1,128)} %get-tuple-element.44) | copy-start | bytes 3076
  109.7 1.0 copy-start.2
  109.7 1.3 copy-start.4
  109.7 1.6 copy-start.6
  109.7 2.0 %copy-start.7 = (f32[32,32,1,256]{3,2,1,0:T(1,128)}, f32[32,32,1,256]{3,2,1,0:T(1,128)S(1)}, u32[]{:S(2)}) copy-start(f32[32,32,1,256]{3,2,1,0:T(1,128)S(1)} %get-tuple-element.18) | copy-start | bytes 3145732
  109.8 2.4 %copy-start.8 = (f32[32,32,1,256]{3,2,1,0:T(1,128)}, f32[32,32,1,256]{3,2,1,0:T(1,128)S(1)}, u32[]{:S(2)}) copy-start(f32[32,32,1,256]{3,2,1,0:T(1,128)S(1)} %get-tuple-element.13) | copy-start | bytes 3145732
  109.8 2.6 %copy-start.9 = (f32[32,32,1,256]{3,2,1,0:T(1,128)}, f32[32,32,1,256]{3,2,1,0:T(1,128)S(1)}, u32[]{:S(2)}) copy-start(f32[32,32,1,256]{3,2,1,0:T(1,128)S(1)} %get-tuple-element.19) | copy-start | bytes 3145732
  109.8 4.6 %copy-start.21 = (f32[8,8,256]{2,1,0:T(8,128)S(1)}, f32[8,8,256]{2,1,0:T(8,128)}, u32[]{:S(2)}) copy-start(f32[8,8,256]{2,1,0:T(8,128)} %constant_dynamic-update-slice_fusion.9) | copy-start | bytes 196612
  109.8 4.6 %copy-start.22 = (f32[1,256]{1,0:T(1,128)S(1)}, f32[1,256]{1,0:T(1,128)}, u32[]{:S(2)}) copy-start(f32[1,256]{1,0:T(1,128)} %get-tuple-element.46) | copy-start | bytes 3076
  109.8 4.6 %copy-start.23 = (f32[1,256]{1,0:T(1,128)S(1)}, f32[1,256]{1,0:T(1,128)}, u32[]{:S(2)}) copy-start(f32[1,256]{1,0:T(1,128)} %get-tuple-element.57) | copy-start | bytes 3076
  109.8 4.6 %copy-start.24 = (f32[1,256]{1,0:T(1,128)S(1)}, f32[1,256]{1,0:T(1,128)}, u32[]{:S(2)}) copy-start(f32[1,256]{1,0:T(1,128)} %get-tuple-element.47) | copy-start | bytes 3076
  109.8 4.6 %copy-start.25 = (f32[8]{0:T(128)S(1)}, f32[8]{0:T(128)}, u32[]{:S(2)}) copy-start(f32[8]{0:T(128)} %get-tuple-element.64) | copy-start | bytes 100
  109.8 4.6 %copy-start.28 = (f32[1,256]{1,0:T(1,128)S(1)}, f32[1,256]{1,0:T(1,128)}, u32[]{:S(2)}) copy-start(f32[1,256]{1,0:T(1,128)} %get-tuple-element.58) | copy-start | bytes 3076
  109.8 4.6 %copy-start.29 = (f32[1,256]{1,0:T(1,128)S(1)}, f32[1,256]{1,0:T(1,128)}, u32[]{:S(2)}) copy-start(f32[1,256]{1,0:T(1,128)} %get-tuple-element.48) | copy-start | bytes 3076
  109.8 4.6 %copy-start.30 = (f32[8]{0:T(128)S(1)}, f32[8]{0:T(128)}, u32[]{:S(2)}) copy-start(f32[8]{0:T(128)} %get-tuple-element.65) | copy-start | bytes 100
  109.9 4.6 %copy-start.31 = (f32[1,256]{1,0:T(1,128)S(1)}, f32[1,256]{1,0:T(1,128)}, u32[]{:S(2)}) copy-start(f32[1,256]{1,0:T(1,128)} %get-tuple-element.59) | copy-start | bytes 3076
  109.9 4.6 %copy-start.32 = (f32[1,256]{1,0:T(1,128)S(1)}, f32[1,256]{1,0:T(1,128)}, u32[]{:S(2)}) copy-start(f32[1,256]{1,0:T(1,128)} %get-tuple-element.49) | copy-start | bytes 3076
  109.9 4.6 %copy-start.33 = (f32[8]{0:T(128)S(1)}, f32[8]{0:T(128)}, u32[]{:S(2)}) copy-start(f32[8]{0:T(128)} %get-tuple-element.66) | copy-start | bytes 100
  109.9 4.6 %copy-start.34 = (f32[8]{0:T(128)S(1)}, f32[8]{0:T(128)}, u32[]{:S(2)}) copy-start(f32[8]{0:T(128)} %get-tuple-element.67) | copy-start | bytes 100
  109.9 4.6 %copy-start.35 = (f32[8]{0:T(128)S(1)}, f32[8]{0:T(128)}, u32[]{:S(2)}) copy-start(f32[8]{0:T(128)} %get-tuple-element.68) | copy-start | bytes 100
  109.9 4.6 %copy-start.36 = (f32[8]{0:T(128)S(1)}, f32[8]{0:T(128)}, u32[]{:S(2)}) copy-start(f32[8]{0:T(128)} %get-tuple-element.69) | copy-start | bytes 100
  109.9 5.3 %copy-start.46 = (f32[1,256]{1,0:T(1,128)S(1)}, f32[1,256]{1,0:T(1,128)}, u32[]{:S(2)}) copy-start(f32[1,256]{1,0:T(1,128)} %get-tuple-element.6) | copy-start | bytes 3076
  109.9 5.3 %copy-start.47 = (f32[1,256]{1,0:T(1,128)S(1)}, f32[1,256]{1,0:T(1,128)}, u32[]{:S(2)}) copy-start(f32[1,256]{1,0:T(1,128)} %get-tuple-element.7) | copy-start | bytes 3076
  109.9 5.3 %copy-start.48 = (f32[1,256]{1,0:T(1,128)S(1)}, f32[1,256]{1,0:T(1,128)}, u32[]{:S(2)}) copy-start(f32[1,256]{1,0:T(1,128)} %get-tuple-element.8) | copy-start | bytes 3076
  109.9 5.3 %copy-start.49 = (f32[1,256]{1,0:T(1,128)S(1)}, f32[1,256]{1,0:T(1,128)}, u32[]{:S(2)}) copy-start(f32[1,256]{1,0:T(1,128)} %get-tuple-element.9) | copy-start | bytes 3076
  110.0 5.3 %copy-start.50 = (f32[1,256]{1,0:T(1,128)S(1)}, f32[1,256]{1,0:T(1,128)}, u32[]{:S(2)}) copy-start(f32[1,256]{1,0:T(1,128)} %get-tuple-element.10) | copy-start | bytes 3076
  110.0 5.3 %copy-start.51 = (f32[1,256]{1,0:T(1,128)S(1)}, f32[1,256]{1,0:T(1,128)}, u32[]{:S(2)}) copy-start(f32[1,256]{1,0:T(1,128)} %get-tuple-element.11) | copy-start | bytes 3076
  110.0 5.3 %copy-start.52 = (f32[1,256]{1,0:T(1,128)S(1)}, f32[1,256]{1,0:T(1,128)}, u32[]{:S(2)}) copy-start(f32[1,256]{1,0:T(1,128)} %get-tuple-element.12) | copy-start | bytes 3076
  116.0 6.5 %copy-start.3 = (f32[32,32,1,256]{3,2,1,0:T(1,128)S(1)}, f32[32,32,1,256]{3,2,1,0:T(1,128)}, u32[]{:S(2)}) copy-start(f32[32,32,1,256]{3,2,1,0:T(1,128)} %copy-done.2) | copy-start | bytes 3145732
  116.0 6.5 %copy-start.5 = (f32[32,32,1,256]{3,2,1,0:T(1,128)S(1)}, f32[32,32,1,256]{3,2,1,0:T(1,128)}, u32[]{:S(2)}) copy-start(f32[32,32,1,256]{3,2,1,0:T(1,128)} %copy-done.4) | copy-start | bytes 3145732
  125.5 26.6 %copy-start.10 = (f32[32,32,256]{2,1,0:T(8,128)S(1)}, f32[32,32,256]{2,1,0:T(8,128)}, u32[]{:S(2)}) copy-start(f32[32,32,256]{2,1,0:T(8,128)} %get-tuple-element.78) | copy-start | bytes 3145732
  125.5 26.6 %copy-start.11 = (f32[32,32,256]{2,1,0:T(8,128)S(1)}, f32[32,32,256]{2,1,0:T(8,128)}, u32[]{:S(2)}) copy-start(f32[32,32,256]{2,1,0:T(8,128)} %get-tuple-element.79) | copy-start | bytes 3145732
  149.2 2.9 %copy-start.12 = (f32[32,32,256]{2,1,0:T(8,128)S(1)}, f32[32,32,256]{2,1,0:T(8,128)}, u32[]{:S(2)}) copy-start(f32[32,32,256]{2,1,0:T(8,128)} %get-tuple-element.76) | copy-start | bytes 3145732
  149.2 2.9 %copy-start.13 = (f32[32,32,256]{2,1,0:T(8,128)S(1)}, f32[32,32,256]{2,1,0:T(8,128)}, u32[]{:S(2)}) copy-start(f32[32,32,256]{2,1,0:T(8,128)} %get-tuple-element.77) | copy-start | bytes 3145732
  149.2 2.9 %copy-start.14 = (f32[32,32,256]{2,1,0:T(8,128)S(1)}, f32[32,32,256]{2,1,0:T(8,128)}, u32[]{:S(2)}) copy-start(f32[32,32,256]{2,1,0:T(8,128)} %get-tuple-element.74) | copy-start | bytes 3145732
  149.2 2.9 %copy-start.15 = (f32[32,32,256]{2,1,0:T(8,128)S(1)}, f32[32,32,256]{2,1,0:T(8,128)}, u32[]{:S(2)}) copy-start(f32[32,32,256]{2,1,0:T(8,128)} %get-tuple-element.75) | copy-start | bytes 3145732
  149.2 3.1 %copy-start.16 = (f32[32,32,256]{2,1,0:T(8,128)S(1)}, f32[32,32,256]{2,1,0:T(8,128)}, u32[]{:S(2)}) copy-start(f32[32,32,256]{2,1,0:T(8,128)} %get-tuple-element.72) | copy-start | bytes 3145732
  149.2 3.4 %copy-start.17 = (f32[32,32,256]{2,1,0:T(8,128)S(1)}, f32[32,32,256]{2,1,0:T(8,128)}, u32[]{:S(2)}) copy-start(f32[32,32,256]{2,1,0:T(8,128)} %get-tuple-element.73) | copy-start | bytes 3145732
Sparse Core Ops, SparseCore 0:
  114.5 34.6 all-gather.1
